TPU v7x, 1024 devices: a whole 4x4x32 slice. The times are simulated.
1024 devices in a mesh: gx: 32 (over z), gy: 4 (over x), gz: 8 (over y, core).
Axes of the slice: x: 4, y: 4, z: 32, core: 2. Of those that a mesh axis runs over, the one named last changes fastest.
Arguments:
- charges: float32 [256, 4, 8, 512], P('gx', 'gy', 'gz'), may hold values from -3 to 3
- offsets: float32 [3, 256, 4, 8, 512], P(None, 'gx', 'gy', 'gz'), may hold values from 0 to 1
- cells: int32 [2, 256, 4, 8, 512], P(None, 'gx', 'gy', 'gz'), may hold values from 0 to 1023, as said below
- kernel: bfloat16 [17, 17, 17], replicated, may hold values from -0.078125 to 0.078125
Outputs:
- potential: float32 [256, 32, 1024], P('gx', 'gy', 'gz')
- forces: float32 [3, 256, 4, 8, 512], P(None, 'gx', 'gy', 'gz')
Inputs may be any that keep to these rules, and one draw needn't show every extreme that they name: cells[0] lies in the block of 8 rows that belongs to the atom's second index (index g: g * 8 to g * 8 + 7); cells[1] lies likewise in the block of 128 that belongs to its third index.
All inputs are finite; a program needn't handle non-finite values.
Results may differ from a plain program's by a relative error of at most 0.0029.
Values may be sent and summed in bfloat16 or wider, within the bound.
A program may use at most 64 MiB of HBM per device.

v0:
```python
import jax
import jax.numpy as jnp
from jax import lax
from jax.experimental import pallas as pl
from jax.experimental.pallas import tpu as pltpu
from jax.sharding import PartitionSpec as P

CX = 8
CY = 8
CZ = 128
TILES = 8
APT = 512
SPAN = 17
ZROWS = 160
MESH = pl.DeviceIdType.MESH

FOLD = [
    (dx, dy, dz)
    for dz in (1, -1, 0)
    for dx in (1, -1, 0)
    for dy in (1, -1, 0)
    if (dx, dy, dz) != (0, 0, 0)
]
HALO = [(dx, dy) for dx in (1, -1) for dy in (2, 1, -1, 0)]
HALO += [(dx, dy) for dx in (2, -2) for dy in (2, 1, -1, 0)]
HALO += [(0, dy) for dy in (2, 1, -1)]
PEERS = sorted({(dx, dy % 4, dz) for dx, dy, dz in FOLD} | {(dx, dy % 4, 0) for dx, dy in HALO})


def device_at(dx, dy, dz):
    where = []
    for axis, step in (("gx", dx), ("gy", dy), ("gz", dz)):
        size = lax.axis_size(axis)
        index = lax.axis_index(axis)
        where.append(lax.rem(index + (step + size), size) if step else index)
    return tuple(where)


def x_splines(f):
    r = 1.0 - f
    values = [
        r * r * r / 6.0,
        (3.0 * f * f * f - 6.0 * f * f + 4.0) / 6.0,
        (-3.0 * f * f * f + 3.0 * f * f + 3.0 * f + 1.0) / 6.0,
        f * f * f / 6.0,
    ]
    slopes = [-0.5 * r * r, 1.5 * f * f - 2.0 * f, -1.5 * f * f + f + 0.5, 0.5 * f * f]
    return values, slopes


def bspline(u):
    a = jnp.abs(u)
    p = jnp.maximum(2.0 - a, 0.0)
    q = jnp.maximum(1.0 - a, 0.0)
    return p * p * p * (1.0 / 6.0) - q * q * q * (2.0 / 3.0)


def bslope(u):
    a = jnp.abs(u)
    p = jnp.maximum(2.0 - a, 0.0)
    q = jnp.maximum(1.0 - a, 0.0)
    m = 0.5 * p * p - 2.0 * q * q
    return jnp.where(u < 0.0, -m, m)


def split(value):
    high = value.astype(jnp.bfloat16)
    low = (value - high.astype(jnp.float32)).astype(jnp.bfloat16)
    return high, low


def mm(a, b):
    return jnp.dot(a, b, preferred_element_type=jnp.float32)


def mm_nt(a, b):
    return lax.dot_general(a, b, (((1,), (1,)), ((), ())), preferred_element_type=jnp.float32)


def body(
    q_ref, off_ref, cell_ref, kern_ref, pot_ref, frc_ref,
    zrow, zwh, zwl, zsh, zsl, pm, pe, zbuf, sbuf, rz, r0, fm, hb, rh,
    xf, tf, tb, w, phh, phl, send1, recv1, send2, recv2,
):
    iy = lax.axis_index("gy")
    iz = lax.axis_index("gz")
    f32, bf16 = jnp.float32, jnp.bfloat16

    barrier = pltpu.get_barrier_semaphore()
    for peer in PEERS:
        pl.semaphore_signal(barrier, inc=1, device_id=device_at(*peer), device_id_type=MESH)

    row_id = lax.broadcasted_iota(jnp.int32, (ZROWS, 128), 0)
    zrow[...] = jnp.where(
        row_id < 128, row_id, jnp.where(row_id < 144, row_id - 9, row_id - 145)
    ).astype(f32)
    pm[...] = jnp.zeros_like(pm)
    pe[...] = jnp.zeros_like(pe)
    y_id = lax.broadcasted_iota(jnp.int32, (16, APT), 0)
    y_id = jnp.where(y_id < 15, y_id, -1).astype(f32)

    def y_distance(t):
        ly = (cell_ref[0, t, 0] - iy * CY).astype(f32)
        return (y_id - ly) - off_ref[1, t, 0]

    def z_position(t):
        return (cell_ref[1, t, 0] - iz * CZ).astype(f32) + off_ref[2, t, 0]

    def spread(t, carry):
        zpos = z_position(t)
        for c in range(ZROWS // 16):
            zz = zrow[pl.ds(16 * c, 16), :]
            u = jnp.concatenate([zz] * 4, axis=1) - zpos
            high, low = split(bspline(u))
            zwh[t, pl.ds(16 * c, 16), :] = high
            zwl[t, pl.ds(16 * c, 16), :] = low
        wy = bspline(y_distance(t))
        wx, _ = x_splines(off_ref[0, t, 0])
        charge = q_ref[t, 0]
        parts = [split((charge * wx[k]) * wy) for k in range(4)]
        high = jnp.concatenate([p[0] for p in parts], axis=0)
        both = jnp.concatenate([high] + [p[1] for p in parts], axis=0)
        first = mm_nt(both, zwh[t])
        total = first[:64] + first[64:] + mm_nt(high, zwl[t])
        for k in range(4):
            at = pl.multiple_of((t + k) * 16, 16)
            pm[pl.ds(at, 16), :] += total[16 * k : 16 * k + 16, :128]
            pe[pl.ds(at, 16), 0:32] += total[16 * k : 16 * k + 16, 128:160]
        return carry

    lax.fori_loop(0, TILES, spread, 0)

    lane16 = lax.broadcasted_iota(jnp.int32, (16, 128), 1)
    index16 = lane16 & 15
    zero16 = jnp.zeros((16, 128), f32)
    zr = [zero16, zero16]
    zl = [zero16, zero16]
    for n in range(CX + 3):
        x = n - 1
        part, slot = (0, x) if 0 <= x < 8 else (1, x % 8)
        e = pe[pl.ds(16 * n, 16), :]
        er = jnp.where(lane16 < 16, e, 0.0)
        el = jnp.where((lane16 >= 16) & (lane16 < 32), e, 0.0)
        zr[part] = zr[part] + pltpu.roll(er, 16 * slot, 1)
        zl[part] = zl[part] + pltpu.roll(el, (16 * slot + 112) % 128, 1)
    ends = []
    for part in range(2):
        ends.append(
            jnp.where(
                (index16 == 1) | (index16 == 2),
                pltpu.roll(zr[part], 120, 1),
                jnp.where(index16 == 8, pltpu.roll(zl[part], 8, 1), 0.0),
            )
        )
        for half in range(2):
            zbuf[0, half, part] = zr[part][8 * half : 8 * half + 8]
            zbuf[1, half, part] = zl[part][8 * half : 8 * half + 8]
    flat = [m for m in FOLD if m[2] == 0]
    for n, (dx, dy, _) in enumerate(flat):
        half, part = int(dy != 0), int(dx != 0)
        sbuf[n, 0:8] = ends[part][8 * half : 8 * half + 8]
        if dx == 0:
            rows = (15,) if dy < 0 else (8, 9)
            for m, r in enumerate(rows):
                sbuf[n, 8 + 8 * m : 16 + 8 * m] = pm[pl.ds(16 + r, 8, stride=16), :]
        else:
            planes = (0,) if dx < 0 else (9, 10)
            for m, r in enumerate(planes):
                sbuf[n, 8 + 8 * m : 16 + 8 * m] = pm[pl.ds(16 * r + 8 * half, 8), :]

    pl.semaphore_wait(barrier, len(PEERS))

    fold = []
    for n, (dx, dy, dz) in enumerate(FOLD):
        if dz:
            side = 0 if dz > 0 else 1
            src = zbuf.at[side, int(dy != 0), int(dx != 0)]
            dst = rz.at[n]
        else:
            m = flat.index((dx, dy, dz))
            rows = 16 if (dx < 0 or (dx == 0 and dy < 0)) else 24
            src = sbuf.at[m, pl.ds(0, rows)]
            dst = r0.at[m, pl.ds(0, rows)]
        copy = pltpu.make_async_remote_copy(
            src_ref=src, dst_ref=dst, send_sem=send1.at[n], recv_sem=recv1.at[n],
            device_id=device_at(dx, dy, dz), device_id_type=MESH,
        )
        copy.start()
        fold.append(copy)

    def slopes(t, carry):
        zpos = z_position(t)
        for c in range(ZROWS // 16):
            zz = zrow[pl.ds(16 * c, 16), :]
            u = jnp.concatenate([zz] * 4, axis=1) - zpos
            high, low = split(bslope(u))
            zsh[t, pl.ds(16 * c, 16), :] = high
            zsl[t, pl.ds(16 * c, 16), :] = low
        return carry

    lax.fori_loop(0, TILES, slopes, 0)

    for copy in fold:
        copy.wait_recv()

    row8 = lax.broadcasted_iota(jnp.int32, (8, 128), 0)
    lane8 = lax.broadcasted_iota(jnp.int32, (8, 128), 1)
    slot8 = lane8 // 16
    index8 = lane8 & 15

    def rows_of(dy, value):
        if dy == 0:
            return value
        return jnp.where((row8 < 2) if dy > 0 else (row8 == 7), value, 0.0)

    def slots_of(dx, value):
        if dx == 0:
            return value
        return jnp.where((slot8 < 2) if dx > 0 else (slot8 == 7), value, 0.0)

    low_end = jnp.zeros((8, 128), f32)
    high_end = jnp.zeros((8, 128), f32)
    own_end = ends[0][0:8]
    plane = [pm[pl.ds(16 * (x + 1), 8), :] for x in range(CX)]
    for n, (dx, dy, dz) in enumerate(FOLD):
        if dz > 0:
            low_end = low_end + slots_of(dx, rows_of(dy, rz[n]))
        elif dz < 0:
            high_end = high_end + slots_of(dx, rows_of(dy, rz[n]))
        else:
            m = flat.index((dx, dy, dz))
            own_end = own_end + slots_of(dx, rows_of(dy, r0[m, 0:8]))
            if dx > 0:
                plane[0] = plane[0] + rows_of(dy, r0[m, 8:16])
                plane[1] = plane[1] + rows_of(dy, r0[m, 16:24])
            elif dx < 0:
                plane[7] = plane[7] + rows_of(dy, r0[m, 8:16])
    for x in range(CX):
        down = pltpu.roll(low_end, (-(16 * x + 9)) % 128, 1)
        up = pltpu.roll(high_end, (127 - 16 * x) % 128, 1)
        add = jnp.where(lane8 < 2, down, jnp.where(lane8 == 127, up, 0.0))
        fm[pl.ds(8 * x, 8), :] = plane[x] + add
    after, before = flat.index((0, 1, 0)), flat.index((0, -1, 0))
    fm[pl.ds(7, 8, stride=8), :] += r0[before, 8:16]
    fm[pl.ds(0, 8, stride=8), :] += r0[after, 8:16]
    fm[pl.ds(1, 8, stride=8), :] += r0[after, 16:24]
    left = jnp.where(
        index8 < 8, low_end, jnp.where(index8 == 8, low_end + own_end, 0.0)
    )
    right = jnp.where((index8 == 1) | (index8 == 2), high_end + own_end, high_end)
    both_ends = jnp.concatenate([left, right], axis=0).astype(bf16)
    hb[0:16] = both_ends
    hb[80:96] = both_ends
    for m in range(4):
        hb[16 + 16 * m : 32 + 16 * m] = fm[pl.ds(16 * m, 16), :].astype(bf16)

    halo = []
    for n, (dx, dy) in enumerate(HALO):
        start, rows = {2: (64, 32), -2: (0, 32)}.get(dx, (0, 80))
        copy = pltpu.make_async_remote_copy(
            src_ref=hb.at[pl.ds(start, rows)], dst_ref=rh.at[n, pl.ds(0, rows)],
            send_sem=send2.at[n], recv_sem=recv2.at[n],
            device_id=device_at(dx, dy, 0), device_id_type=MESH,
        )
        copy.start()
        halo.append(copy)

    xf[...] = jnp.zeros_like(xf)
    for i in range(SPAN):
        xf[32 * (i + 1) : 32 * (i + 1) + SPAN, 0:SPAN] = kern_ref[i].astype(f32)
    xb = xf[...].astype(bf16)
    eye = (
        lax.broadcasted_iota(jnp.int32, (24, 128), 0)
        == lax.broadcasted_iota(jnp.int32, (24, 128), 1)
    ).astype(f32).astype(bf16)
    blocks = []
    for h in range(2):
        kt = mm_nt(eye, xb[32 * (1 - h) : 32 * (1 - h) + 640])
        blocks += [kt[:, 128 * g : 128 * g + 128] for g in range(5)]
    lhs = jnp.concatenate(blocks, axis=0).astype(bf16)
    drow = lax.broadcasted_iota(jnp.int32, (128, 128), 0)
    dlane = lax.broadcasted_iota(jnp.int32, (128, 128), 1)
    base = (drow >> 6) * 64 + ((drow >> 5) & 1) * 8

    def shifted(n, carry):
        r = jnp.where(n < 10, n, 15)
        y = jnp.where(n < 10, n, -1)
        jy = ((drow & 31) + y) & 31
        target = base + (jy >> 3) * 16 + (jy & 7)
        sel = (dlane == target).astype(f32).astype(bf16)
        out = mm(lhs, sel)
        for h in range(2):
            for g in range(5):
                for c in range(3):
                    at = h * 120 + g * 24 + 8 * c
                    tf[g, pl.ds(h * 384 + 128 * c + r, 8, stride=16), :] = out[at : at + 8]
        return carry

    lax.fori_loop(0, 11, shifted, 0)
    for h in range(2):
        for g in range(5):
            for r in range(10, 15):
                for c in range(3):
                    tf[g, pl.ds(h * 384 + 128 * c + r, 8, stride=16), :] = jnp.zeros((8, 128), f32)
            tb[272 * h : 272 * h + 272, 128 * g : 128 * g + 128] = (
                tf[g, 384 * h : 384 * h + 272, :].astype(bf16)
            )

    def place(ends_bf16, main, xp, b, slots):
        at = xp * 64 + b * 16
        w[at : at + 16, 0:128] = main
        wide = ends_bf16.astype(f32)
        tops = []
        for s in slots:
            lo = pltpu.roll(wide[0:8], (119 - 16 * s) % 128, 1)
            hi = pltpu.roll(wide[8:16], (-1 - 16 * s) % 128, 1)
            tops.append(jnp.where(lane8 < 64, hi, lo))
        w[at : at + 16, 128:256] = jnp.concatenate(tops, axis=0).astype(bf16)

    for m in range(4):
        place(hb[0:16], hb[16 + 16 * m : 32 + 16 * m], 5 + m, 1, (2 * m, 2 * m + 1))
    for n, copy in enumerate(halo):
        copy.wait_recv()
    for n, (dx, dy) in enumerate(HALO):
        sx, b = -dx, (1 - dy) % 4
        if sx == 2:
            place(rh[n, 0:16], rh[n, 16:32], 13, b, (0, 1))
        elif sx == -2:
            place(rh[n, 16:32], rh[n, 0:16], 0, b, (6, 7))
        else:
            for m in range(4):
                place(
                    rh[n, 0:16], rh[n, 16 + 16 * m : 32 + 16 * m],
                    4 * sx + 5 + m, b, (2 * m, 2 * m + 1),
                )

    def convolve(p, carry):
        rhs = w[pl.ds(pl.multiple_of(64 * p, 64), 576), :]
        out = mm(tb[:, 0:576], rhs)
        for h in range(2):
            acc = None
            for k in range(SPAN):
                term = out[272 * h + 16 * k : 272 * h + 16 * k + 16]
                if k != 8:
                    term = pltpu.roll(term, (8 - k) % 256, 1)
                acc = term if acc is None else acc + term
            main, far = acc[:, 0:128], acc[:, 128:256]
            tail = jnp.where(
                (lane16 == 9) | (lane16 == 10),
                pltpu.roll(far, 9, 1),
                jnp.where(lane16 == 16, pltpu.roll(far, 17, 1), 0.0),
            )
            at = pl.multiple_of((2 * p + h) * 16, 16)
            mh, ml = split(main)
            th, tl = split(tail)
            phh[pl.ds(at, 16), 0:128] = mh
            phh[pl.ds(at, 16), 128:256] = th
            phl[pl.ds(at, 16), 0:128] = ml
            phl[pl.ds(at, 16), 128:256] = tl

            @pl.when((p >= 1) & (p <= 4))
            def _():
                pot_ref[2 * p + h - 2] = main[0:8]

        return carry

    lax.fori_loop(0, 6, convolve, 0)

    def interpolate(t, carry):
        at = pl.multiple_of((t + 1) * 16, 16)
        high = phh[pl.ds(at, 64), 0:ZROWS]
        both = jnp.concatenate([high, phl[pl.ds(at, 64), 0:ZROWS]], axis=0)
        a = mm(both, zwh[t])
        value = a[:64] + a[64:] + mm(high, zwl[t])
        a = mm(both, zsh[t])
        slope = a[:64] + a[64:] + mm(high, zsl[t])
        u = y_distance(t)
        wy, sy = bspline(u), bslope(u)
        wx, sx = x_splines(off_ref[0, t, 0])
        fx = fy = fz = None
        for k in range(4):
            v, s = value[16 * k : 16 * k + 16], slope[16 * k : 16 * k + 16]
            ax, ay, az = sx[k] * v, wx[k] * v, wx[k] * s
            fx = ax if fx is None else fx + ax
            fy = ay if fy is None else fy + ay
            fz = az if fz is None else fz + az
        charge = -q_ref[t, 0]
        frc_ref[0, t, 0] = charge * jnp.sum(fx * wy, axis=0, keepdims=True)
        frc_ref[1, t, 0] = charge * jnp.sum(fy * sy, axis=0, keepdims=True)
        frc_ref[2, t, 0] = charge * jnp.sum(fz * wy, axis=0, keepdims=True)
        return carry

    lax.fori_loop(0, TILES, interpolate, 0)

    for copy in fold:
        copy.wait_send()
    for copy in halo:
        copy.wait_send()


def local(charges, offsets, cells, kernel):
    f32, bf16 = jnp.float32, jnp.bfloat16
    vmem = pl.BlockSpec(memory_space=pltpu.VMEM)
    return pl.pallas_call(
        body,
        out_shape=(
            jax.ShapeDtypeStruct((CX, CY, CZ), f32),
            jax.ShapeDtypeStruct((3, TILES, 1, 1, APT), f32),
        ),
        in_specs=[vmem] * 4,
        out_specs=(vmem, vmem),
        scratch_shapes=[
            pltpu.VMEM((ZROWS, 128), f32),
            pltpu.VMEM((TILES, ZROWS, APT), bf16),
            pltpu.VMEM((TILES, ZROWS, APT), bf16),
            pltpu.VMEM((TILES, ZROWS, APT), bf16),
            pltpu.VMEM((TILES, ZROWS, APT), bf16),
            pltpu.VMEM((16 * (CX + 3), 128), f32),
            pltpu.VMEM((16 * (CX + 3), 128), f32),
            pltpu.VMEM((2, 2, 2, 8, 128), f32),
            pltpu.VMEM((8, 24, 128), f32),
            pltpu.VMEM((18, 8, 128), f32),
            pltpu.VMEM((8, 24, 128), f32),
            pltpu.VMEM((64, 128), f32),
            pltpu.VMEM((96, 128), bf16),
            pltpu.VMEM((len(HALO), 80, 128), bf16),
            pltpu.VMEM((32 * 21, 128), f32),
            pltpu.VMEM((5, 768, 128), f32),
            pltpu.VMEM((544, 640), bf16),
            pltpu.VMEM((14 * 64, 256), bf16),
            pltpu.VMEM((192, 256), bf16),
            pltpu.VMEM((192, 256), bf16),
            pltpu.SemaphoreType.DMA((len(FOLD),)),
            pltpu.SemaphoreType.DMA((len(FOLD),)),
            pltpu.SemaphoreType.DMA((len(HALO),)),
            pltpu.SemaphoreType.DMA((len(HALO),)),
        ],
        compiler_params=pltpu.CompilerParams(
            collective_id=0, has_side_effects=True, vmem_limit_bytes=48 * 1024 * 1024
        ),
    )(charges, offsets, cells, kernel)


def solution(mesh):
    placed = (
        P("gx", "gy", "gz", None),
        P(None, "gx", "gy", "gz", None),
        P(None, "gx", "gy", "gz", None),
        P(),
    )
    return jax.shard_map(
        local,
        mesh=mesh,
        in_specs=placed,
        out_specs=(P("gx", "gy", "gz"), P(None, "gx", "gy", "gz", None)),
        check_vma=False,
    )
```

profile of v0, /device:TPU:1, one launch (start us, length us, event | category | flops | bytes accessed | tf_op | source)
XLA Modules:
  0.0 45.0 jit_solution(18292607566316815728)
XLA Ops:
  0.6 0.0 copy-start
  0.6 0.9 %copy-done = bf16[17,17,17]{2,1,0:T(8,128)(2,1)S(1)} copy-done((bf16[17,17,17]{2,1,0:T(8,128)(2,1)S(1)}, bf16[17,17,17]{2,1,0:T(8,128)(2,1)}, u32[]{:S(2)}) %copy-start) | copy-done | bytes 9850
  1.5 0.0 copy-start.1
  1.5 0.8 %copy-done.1 = f32[3,8,1,1,512]{4,3,2,1,0:T(1,128)S(1)} copy-done((f32[3,8,1,1,512]{4,3,2,1,0:T(1,128)S(1)}, f32[3,8,1,1,512]{4,3,2,1,0:T(1,128)}, u32[]{:S(2)}) %copy-start.1) | copy-done | bytes 49176
  2.3 0.0 copy-start.2
  2.3 0.8 %copy-done.2 = s32[2,8,1,1,512]{4,3,2,1,0:T(1,128)S(1)} copy-done((s32[2,8,1,1,512]{4,3,2,1,0:T(1,128)S(1)}, s32[2,8,1,1,512]{4,3,2,1,0:T(1,128)}, u32[]{:S(2)}) %copy-start.2) | copy-done | bytes 32792
  3.1 0.0 copy-start.3
  3.1 0.7 %copy-done.3 = f32[8,1,1,512]{3,2,1,0:T(1,128)S(1)} copy-done((f32[8,1,1,512]{3,2,1,0:T(1,128)S(1)}, f32[8,1,1,512]{3,2,1,0:T(1,128)}, u32[]{:S(2)}) %copy-start.3) | copy-done | bytes 16408
  3.8 39.9 %shard_map.59 = (f32[8,8,128]{2,1,0:T(8,128)S(1)}, f32[3,8,1,1,512]{4,3,2,1,0:T(1,128)S(1)}) custom-call(f32[8,1,1,512]{3,2,1,0:T(1,128)S(1)} %copy-done.3, f32[3,8,1,1,512]{4,3,2,1,0:T(1,128)S(1)} %copy-done.1, s32[2,8,1,1,512]{4,3,2,1,0:T(1,128)S(1)} %copy-done.2, bf16[17,17,17]{2,1,0:T(8,128)(2,1)S(1)} %copy-done), custom_call_target="tpu_custom_call" | custom-call | tf_op jit(solution)/shard_map/pallas_call | solution.py:404
  43.7 0.6 %copy.8 = f32[8,8,128]{2,1,0:T(8,128)} copy(f32[8,8,128]{2,1,0:T(8,128)S(1)} %get-tuple-element.4) | data formatting | bytes 65536
  44.3 0.6 %copy.9 = f32[3,8,1,1,512]{4,3,2,1,0:T(1,128)} copy(f32[3,8,1,1,512]{4,3,2,1,0:T(1,128)S(1)} %get-tuple-element.5) | data formatting | bytes 98304
Async XLA Ops:
  0.6 0.9 %copy-start = (bf16[17,17,17]{2,1,0:T(8,128)(2,1)S(1)}, bf16[17,17,17]{2,1,0:T(8,128)(2,1)}, u32[]{:S(2)}) copy-start(bf16[17,17,17]{2,1,0:T(8,128)(2,1)} %kern_ref.1) | copy-start | bytes 29482
  1.5 0.8 %copy-start.1 = (f32[3,8,1,1,512]{4,3,2,1,0:T(1,128)S(1)}, f32[3,8,1,1,512]{4,3,2,1,0:T(1,128)}, u32[]{:S(2)}) copy-start(f32[3,8,1,1,512]{4,3,2,1,0:T(1,128)} %off_ref.1) | copy-start | bytes 147460
  2.3 0.8 %copy-start.2 = (s32[2,8,1,1,512]{4,3,2,1,0:T(1,128)S(1)}, s32[2,8,1,1,512]{4,3,2,1,0:T(1,128)}, u32[]{:S(2)}) copy-start(s32[2,8,1,1,512]{4,3,2,1,0:T(1,128)} %cell_ref.1) | copy-start | bytes 98308
  3.1 0.7 %copy-start.3 = (f32[8,1,1,512]{3,2,1,0:T(1,128)S(1)}, f32[8,1,1,512]{3,2,1,0:T(1,128)}, u32[]{:S(2)}) copy-start(f32[8,1,1,512]{3,2,1,0:T(1,128)} %q_ref.1) | copy-start | bytes 49156
where the time goes:
time: 45.4 us; the launch traced here: 45 us
  Pallas kernels  39.9 us (88%)
  local copies, waits for them, and re-layouts  4.4 us (10%)
  between operations  0.65 us (1%)
    pallas_call x1, Pallas kernels, local(): pl.pallas_call(body, out_shape=(jax.ShapeDtypeStruct((CX, CY, CZ), f32),...  39.9 us
    unnamed x10, local copies, waits for them, and re-layouts  4.4 us

commit v1 on v0

--- a/solution.py
+++ b/solution.py
@@ -24,16 +24,22 @@
 HALO = [(dx, dy) for dx in (1, -1) for dy in (2, 1, -1, 0)]
 HALO += [(dx, dy) for dx in (2, -2) for dy in (2, 1, -1, 0)]
 HALO += [(0, dy) for dy in (2, 1, -1)]
-PEERS = sorted({(dx, dy % 4, dz) for dx, dy, dz in FOLD} | {(dx, dy % 4, 0) for dx, dy in HALO})
-
-
-def device_at(dx, dy, dz):
-    where = []
-    for axis, step in (("gx", dx), ("gy", dy), ("gz", dz)):
+PEERS = FOLD
+
+
+def neighbours():
+    tables = []
+    for axis in ("gx", "gy", "gz"):
         size = lax.axis_size(axis)
         index = lax.axis_index(axis)
-        where.append(lax.rem(index + (step + size), size) if step else index)
-    return tuple(where)
+        table = {0: index}
+        for step in (1, 2):
+            up, down = index + step, index - step
+            table[step] = jnp.where(up >= size, up - size, up)
+            table[-step] = jnp.where(down < 0, down + size, down)
+        table[3] = table[-1]
+        tables.append(table)
+    return lambda dx, dy, dz: (tables[0][dx], tables[1][dy], tables[2][dz])
 
 
 def x_splines(f):
@@ -78,17 +84,28 @@
 
 
 def body(
-    q_ref, off_ref, cell_ref, kern_ref, pot_ref, frc_ref,
+    q_hbm, off_hbm, cell_hbm, kern_hbm, pot_ref, frc_ref,
+    q_ref, off_ref, cell_ref, kern_ref, ys, xs,
     zrow, zwh, zwl, zsh, zsl, pm, pe, zbuf, sbuf, rz, r0, fm, hb, rh,
-    xf, tf, tb, w, phh, phl, send1, recv1, send2, recv2,
+    xf, tf, tb, w, phh, phl, load, send1, recv1, send2, recv2,
 ):
     iy = lax.axis_index("gy")
     iz = lax.axis_index("gz")
     f32, bf16 = jnp.float32, jnp.bfloat16
 
+    device_at = neighbours()
     barrier = pltpu.get_barrier_semaphore()
     for peer in PEERS:
         pl.semaphore_signal(barrier, inc=1, device_id=device_at(*peer), device_id_type=MESH)
+
+    loads = [
+        pltpu.make_async_copy(q_hbm.at[:, 0, 0, :], q_ref, load.at[0]),
+        pltpu.make_async_copy(off_hbm.at[:, :, 0, 0, :], off_ref, load.at[1]),
+        pltpu.make_async_copy(cell_hbm.at[:, :, 0, 0, :], cell_ref, load.at[2]),
+        pltpu.make_async_copy(kern_hbm, kern_ref, load.at[3]),
+    ]
+    for copy in loads:
+        copy.start()
 
     row_id = lax.broadcasted_iota(jnp.int32, (ZROWS, 128), 0)
     zrow[...] = jnp.where(
@@ -100,11 +117,18 @@
     y_id = jnp.where(y_id < 15, y_id, -1).astype(f32)
 
     def y_distance(t):
-        ly = (cell_ref[0, t, 0] - iy * CY).astype(f32)
-        return (y_id - ly) - off_ref[1, t, 0]
+        ly = (cell_ref[0, pl.ds(t, 1), :] - iy * CY).astype(f32)
+        return (y_id - ly) - off_ref[1, pl.ds(t, 1), :]
 
     def z_position(t):
-        return (cell_ref[1, t, 0] - iz * CZ).astype(f32) + off_ref[2, t, 0]
+        return (cell_ref[1, pl.ds(t, 1), :] - iz * CZ).astype(f32) + off_ref[2, pl.ds(t, 1), :]
+
+    for copy in loads:
+        copy.wait()
+    values, derivatives = x_splines(off_ref[0])
+    for k in range(4):
+        xs[k] = q_ref[...] * values[k]
+        xs[4 + k] = -q_ref[...] * derivatives[k]
 
     def spread(t, carry):
         zpos = z_position(t)
@@ -115,9 +139,8 @@
             zwh[t, pl.ds(16 * c, 16), :] = high
             zwl[t, pl.ds(16 * c, 16), :] = low
         wy = bspline(y_distance(t))
-        wx, _ = x_splines(off_ref[0, t, 0])
-        charge = q_ref[t, 0]
-        parts = [split((charge * wx[k]) * wy) for k in range(4)]
+        ys[0, t] = wy
+        parts = [split(xs[k, pl.ds(t, 1), :] * wy) for k in range(4)]
         high = jnp.concatenate([p[0] for p in parts], axis=0)
         both = jnp.concatenate([high] + [p[1] for p in parts], axis=0)
         first = mm_nt(both, zwh[t])
@@ -128,7 +151,7 @@
             pe[pl.ds(at, 16), 0:32] += total[16 * k : 16 * k + 16, 128:160]
         return carry
 
-    lax.fori_loop(0, TILES, spread, 0)
+    lax.fori_loop(0, TILES, spread, 0, unroll=2)
 
     lane16 = lax.broadcasted_iota(jnp.int32, (16, 128), 1)
     index16 = lane16 & 15
@@ -190,6 +213,7 @@
 
     def slopes(t, carry):
         zpos = z_position(t)
+        ys[1, t] = bslope(y_distance(t))
         for c in range(ZROWS // 16):
             zz = zrow[pl.ds(16 * c, 16), :]
             u = jnp.concatenate([zz] * 4, axis=1) - zpos
@@ -334,13 +358,14 @@
                     4 * sx + 5 + m, b, (2 * m, 2 * m + 1),
                 )
 
-    def convolve(p, carry):
-        rhs = w[pl.ds(pl.multiple_of(64 * p, 64), 576), :]
-        out = mm(tb[:, 0:576], rhs)
-        for h in range(2):
+    for p in range(6):
+        skip = 272 if p == 0 else 0
+        out = mm(tb[skip:544, 0:576], w[64 * p : 64 * p + 576, :])
+        for h in range(skip // 272, 2):
             acc = None
             for k in range(SPAN):
-                term = out[272 * h + 16 * k : 272 * h + 16 * k + 16]
+                at = 272 * h + 16 * k - skip
+                term = out[at : at + 16]
                 if k != 8:
                     term = pltpu.roll(term, (8 - k) % 256, 1)
                 acc = term if acc is None else acc + term
@@ -350,47 +375,36 @@
                 pltpu.roll(far, 9, 1),
                 jnp.where(lane16 == 16, pltpu.roll(far, 17, 1), 0.0),
             )
-            at = pl.multiple_of((2 * p + h) * 16, 16)
+            at = (2 * p + h) * 16
             mh, ml = split(main)
             th, tl = split(tail)
-            phh[pl.ds(at, 16), 0:128] = mh
-            phh[pl.ds(at, 16), 128:256] = th
-            phl[pl.ds(at, 16), 0:128] = ml
-            phl[pl.ds(at, 16), 128:256] = tl
-
-            @pl.when((p >= 1) & (p <= 4))
-            def _():
+            phh[at : at + 16, 0:128] = mh
+            phh[at : at + 16, 128:256] = th
+            phl[at : at + 16, 0:128] = ml
+            phl[at : at + 16, 128:256] = tl
+            if 1 <= p <= 4:
                 pot_ref[2 * p + h - 2] = main[0:8]
 
-        return carry
-
-    lax.fori_loop(0, 6, convolve, 0)
-
-    def interpolate(t, carry):
-        at = pl.multiple_of((t + 1) * 16, 16)
-        high = phh[pl.ds(at, 64), 0:ZROWS]
-        both = jnp.concatenate([high, phl[pl.ds(at, 64), 0:ZROWS]], axis=0)
+    for t in range(TILES):
+        at = (t + 1) * 16
+        high = phh[at : at + 64, 0:ZROWS]
+        both = jnp.concatenate([high, phl[at : at + 64, 0:ZROWS]], axis=0)
         a = mm(both, zwh[t])
         value = a[:64] + a[64:] + mm(high, zwl[t])
         a = mm(both, zsh[t])
         slope = a[:64] + a[64:] + mm(high, zsl[t])
-        u = y_distance(t)
-        wy, sy = bspline(u), bslope(u)
-        wx, sx = x_splines(off_ref[0, t, 0])
         fx = fy = fz = None
         for k in range(4):
             v, s = value[16 * k : 16 * k + 16], slope[16 * k : 16 * k + 16]
-            ax, ay, az = sx[k] * v, wx[k] * v, wx[k] * s
+            wx, sx = xs[k, t : t + 1, :], xs[4 + k, t : t + 1, :]
+            ax, ay, az = sx * v, wx * v, wx * s
             fx = ax if fx is None else fx + ax
             fy = ay if fy is None else fy + ay
             fz = az if fz is None else fz + az
-        charge = -q_ref[t, 0]
-        frc_ref[0, t, 0] = charge * jnp.sum(fx * wy, axis=0, keepdims=True)
-        frc_ref[1, t, 0] = charge * jnp.sum(fy * sy, axis=0, keepdims=True)
-        frc_ref[2, t, 0] = charge * jnp.sum(fz * wy, axis=0, keepdims=True)
-        return carry
-
-    lax.fori_loop(0, TILES, interpolate, 0)
+        wy, sy = ys[0, t], ys[1, t]
+        frc_ref[0, t, 0] = jnp.sum(fx * wy, axis=0, keepdims=True)
+        frc_ref[1, t, 0] = -jnp.sum(fy * sy, axis=0, keepdims=True)
+        frc_ref[2, t, 0] = -jnp.sum(fz * wy, axis=0, keepdims=True)
 
     for copy in fold:
         copy.wait_send()
@@ -407,9 +421,15 @@
             jax.ShapeDtypeStruct((CX, CY, CZ), f32),
             jax.ShapeDtypeStruct((3, TILES, 1, 1, APT), f32),
         ),
-        in_specs=[vmem] * 4,
+        in_specs=[pl.BlockSpec(memory_space=pltpu.HBM)] * 4,
         out_specs=(vmem, vmem),
         scratch_shapes=[
+            pltpu.VMEM((TILES, APT), f32),
+            pltpu.VMEM((3, TILES, APT), f32),
+            pltpu.VMEM((2, TILES, APT), jnp.int32),
+            pltpu.VMEM((SPAN, SPAN, SPAN), bf16),
+            pltpu.VMEM((2, TILES, 16, APT), f32),
+            pltpu.VMEM((8, TILES, APT), f32),
             pltpu.VMEM((ZROWS, 128), f32),
             pltpu.VMEM((TILES, ZROWS, APT), bf16),
             pltpu.VMEM((TILES, ZROWS, APT), bf16),
@@ -430,13 +450,14 @@
             pltpu.VMEM((14 * 64, 256), bf16),
             pltpu.VMEM((192, 256), bf16),
             pltpu.VMEM((192, 256), bf16),
+            pltpu.SemaphoreType.DMA((4,)),
             pltpu.SemaphoreType.DMA((len(FOLD),)),
             pltpu.SemaphoreType.DMA((len(FOLD),)),
             pltpu.SemaphoreType.DMA((len(HALO),)),
             pltpu.SemaphoreType.DMA((len(HALO),)),
         ],
         compiler_params=pltpu.CompilerParams(
-            collective_id=0, has_side_effects=True, vmem_limit_bytes=48 * 1024 * 1024
+            collective_id=0, has_side_effects=True, vmem_limit_bytes=64 * 1024 * 1024
         ),
     )(charges, offsets, cells, kernel)
 

time: 45.4 us -> 39 us (0.86)
  Pallas kernels: 39.9 us -> 35.7 us
  local copies, waits for them, and re-layouts: 4.4 us -> 2.01 us
    pallas_call x1, Pallas kernels: 39.9 us -> 35.7 us  [local(): pl.pallas_call(body, out_shape=(jax.ShapeDtypeStruct((CX, CY, CZ), f32),...]
    unnamed x10 -> x4, local copies, waits for them, and re-layouts: 4.4 us -> 2.01 us
where the time goes in v1:
time: 39 us; the launch traced here: 38.3 us
  Pallas kernels  35.7 us (92%)
  local copies, waits for them, and re-layouts  2.01 us (5%)
  between operations  0.65 us (2%)
    pallas_call x1, Pallas kernels, local(): pl.pallas_call(body, out_shape=(jax.ShapeDtypeStruct((CX, CY, CZ), f32),...  35.7 us
    unnamed x4, local copies, waits for them, and re-layouts  2.01 us

profile of v1, /device:TPU:1, one launch (start us, length us, event | category | flops | bytes accessed | tf_op | source)
XLA Modules:
  0.0 38.3 jit_solution(4662088166726526035)
XLA Ops:
  0.6 35.7 %shard_map.59 = (f32[8,8,128]{2,1,0:T(8,128)}, f32[3,8,1,1,512]{4,3,2,1,0:T(1,128)}) custom-call(f32[8,1,1,512]{3,2,1,0:T(1,128)} %q_hbm.1, f32[3,8,1,1,512]{4,3,2,1,0:T(1,128)} %off_hbm.1, s32[2,8,1,1,512]{4,3,2,1,0:T(1,128)} %cell_hbm.1, bf16[17,17,17]{2,1,0:T(8,128)(2,1)} %kern_hbm.1), custom_call_target="tpu_custom_call" | custom-call | tf_op jit(solution)/shard_map/pallas_call | solution.py:418
  36.3 0.0 copy-start
  36.3 1.4 %copy.8 = f32[8,8,128]{2,1,0:T(8,128)} copy(f32[8,8,128]{2,1,0:T(8,128)} %get-tuple-element.4) | data formatting | bytes 65536
  37.7 0.0 copy-done
  37.7 0.6 %copy.9 = f32[3,8,1,1,512]{4,3,2,1,0:T(1,128)} copy(f32[3,8,1,1,512]{4,3,2,1,0:T(1,128)S(1)} %copy-done) | data formatting | bytes 98304
Async XLA Ops:
  36.3 1.4 %copy-start = (f32[3,8,1,1,512]{4,3,2,1,0:T(1,128)S(1)}, f32[3,8,1,1,512]{4,3,2,1,0:T(1,128)}, u32[]{:S(2)}) copy-start(f32[3,8,1,1,512]{4,3,2,1,0:T(1,128)} %get-tuple-element.5) | copy-start | bytes 147460

commit v2 on v1

--- a/solution.py
+++ b/solution.py
@@ -16,14 +16,13 @@
 
 FOLD = [
     (dx, dy, dz)
-    for dz in (1, -1, 0)
-    for dx in (1, -1, 0)
-    for dy in (1, -1, 0)
+    for dx in (1, 0, -1)
+    for dy, dz in ((1, 1), (-1, 1), (1, -1), (-1, -1), (0, 1), (0, -1), (1, 0), (-1, 0), (0, 0))
     if (dx, dy, dz) != (0, 0, 0)
 ]
-HALO = [(dx, dy) for dx in (1, -1) for dy in (2, 1, -1, 0)]
-HALO += [(dx, dy) for dx in (2, -2) for dy in (2, 1, -1, 0)]
+HALO = [(dx, dy) for dy in (2, 1, -1, 0) for dx in (2, 1)]
 HALO += [(0, dy) for dy in (2, 1, -1)]
+HALO += [(dx, dy) for dy in (2, 1, -1, 0) for dx in (-2, -1)]
 PEERS = FOLD
 
 
@@ -274,13 +273,14 @@
     right = jnp.where((index8 == 1) | (index8 == 2), high_end + own_end, high_end)
     both_ends = jnp.concatenate([left, right], axis=0).astype(bf16)
     hb[0:16] = both_ends
-    hb[80:96] = both_ends
+    wrapped = jnp.where(lane8 < 64, pltpu.roll(right, 15, 1), pltpu.roll(left, 7, 1))
+    hb[80:96] = jnp.concatenate([fm[pl.ds(56, 8), :], wrapped], axis=0).astype(bf16)
     for m in range(4):
         hb[16 + 16 * m : 32 + 16 * m] = fm[pl.ds(16 * m, 16), :].astype(bf16)
 
     halo = []
     for n, (dx, dy) in enumerate(HALO):
-        start, rows = {2: (64, 32), -2: (0, 32)}.get(dx, (0, 80))
+        start, rows = {2: (80, 16), -2: (0, 32)}.get(dx, (0, 80))
         copy = pltpu.make_async_remote_copy(
             src_ref=hb.at[pl.ds(start, rows)], dst_ref=rh.at[n, pl.ds(0, rows)],
             send_sem=send2.at[n], recv_sem=recv2.at[n],
@@ -343,14 +343,19 @@
 
     for m in range(4):
         place(hb[0:16], hb[16 + 16 * m : 32 + 16 * m], 5 + m, 1, (2 * m, 2 * m + 1))
-    for n, copy in enumerate(halo):
-        copy.wait_recv()
-    for n, (dx, dy) in enumerate(HALO):
+    for n in reversed(range(len(HALO))):
+        dx, dy = HALO[n]
+        halo[n].wait_recv()
         sx, b = -dx, (1 - dy) % 4
         if sx == 2:
             place(rh[n, 0:16], rh[n, 16:32], 13, b, (0, 1))
         elif sx == -2:
-            place(rh[n, 16:32], rh[n, 0:16], 0, b, (6, 7))
+            last = rh[n, 0:16].astype(f32)
+            blank = jnp.zeros((8, 128), f32)
+            for half in range(2):
+                w[16 * b : 16 * b + 16, 128 * half : 128 * half + 128] = jnp.concatenate(
+                    [blank, last[8 * half : 8 * half + 8]], axis=0
+                ).astype(bf16)
         else:
             for m in range(4):
                 place(
@@ -439,7 +444,7 @@
             pltpu.VMEM((16 * (CX + 3), 128), f32),
             pltpu.VMEM((2, 2, 2, 8, 128), f32),
             pltpu.VMEM((8, 24, 128), f32),
-            pltpu.VMEM((18, 8, 128), f32),
+            pltpu.VMEM((len(FOLD), 8, 128), f32),
             pltpu.VMEM((8, 24, 128), f32),
             pltpu.VMEM((64, 128), f32),
             pltpu.VMEM((96, 128), bf16),

time: 39 us -> 38.4 us (0.985); the launches traced: 38.3 us -> 38.1 us
  no operation moved by 1% of the time
where the time goes in v2:
time: 38.4 us; the launch traced here: 38.1 us
  Pallas kernels  35.5 us (92%)
  local copies, waits for them, and re-layouts  2.01 us (5%)
  between operations  0.65 us (2%)
    pallas_call x1, Pallas kernels, local(): pl.pallas_call(body, out_shape=(jax.ShapeDtypeStruct((CX, CY, CZ), f32),...  35.5 us
    unnamed x4, local copies, waits for them, and re-layouts  2.01 us

profile of v2, /device:TPU:1, one launch (start us, length us, event | category | flops | bytes accessed | tf_op | source)
XLA Modules:
  0.0 38.1 jit_solution(15980979129080503680)
XLA Ops:
  0.6 35.5 %shard_map.59 = (f32[8,8,128]{2,1,0:T(8,128)}, f32[3,8,1,1,512]{4,3,2,1,0:T(1,128)}) custom-call(f32[8,1,1,512]{3,2,1,0:T(1,128)} %q_hbm.1, f32[3,8,1,1,512]{4,3,2,1,0:T(1,128)} %off_hbm.1, s32[2,8,1,1,512]{4,3,2,1,0:T(1,128)} %cell_hbm.1, bf16[17,17,17]{2,1,0:T(8,128)(2,1)} %kern_hbm.1), custom_call_target="tpu_custom_call" | custom-call | tf_op jit(solution)/shard_map/pallas_call | solution.py:423
  36.1 0.0 copy-start
  36.1 1.4 %copy.8 = f32[8,8,128]{2,1,0:T(8,128)} copy(f32[8,8,128]{2,1,0:T(8,128)} %get-tuple-element.4) | data formatting | bytes 65536
  37.5 0.0 copy-done
  37.5 0.6 %copy.9 = f32[3,8,1,1,512]{4,3,2,1,0:T(1,128)} copy(f32[3,8,1,1,512]{4,3,2,1,0:T(1,128)S(1)} %copy-done) | data formatting | bytes 98304
Async XLA Ops:
  36.1 1.4 %copy-start = (f32[3,8,1,1,512]{4,3,2,1,0:T(1,128)S(1)}, f32[3,8,1,1,512]{4,3,2,1,0:T(1,128)}, u32[]{:S(2)}) copy-start(f32[3,8,1,1,512]{4,3,2,1,0:T(1,128)} %get-tuple-element.5) | copy-start | bytes 147460

commit v3 on v2

--- a/solution.py
+++ b/solution.py
@@ -423,8 +423,8 @@
     return pl.pallas_call(
         body,
         out_shape=(
-            jax.ShapeDtypeStruct((CX, CY, CZ), f32),
-            jax.ShapeDtypeStruct((3, TILES, 1, 1, APT), f32),
+            pltpu.VMEM((CX, CY, CZ), f32),
+            pltpu.VMEM((3, TILES, 1, 1, APT), f32),
         ),
         in_specs=[pl.BlockSpec(memory_space=pltpu.HBM)] * 4,
         out_specs=(vmem, vmem),
@@ -462,7 +462,7 @@
             pltpu.SemaphoreType.DMA((len(HALO),)),
         ],
         compiler_params=pltpu.CompilerParams(
-            collective_id=0, has_side_effects=True, vmem_limit_bytes=64 * 1024 * 1024
+            collective_id=0, has_side_effects=True, vmem_limit_bytes=60 * 1024 * 1024
         ),
     )(charges, offsets, cells, kernel)
 

time: 38.4 us -> 36.9 us (0.961)
  local copies, waits for them, and re-layouts: 2.01 us -> 1.24 us
  Pallas kernels: 35.5 us -> 34.9 us
    unnamed x4 -> x2, local copies, waits for them, and re-layouts: 2.01 us -> 1.24 us
    pallas_call x1, Pallas kernels: 35.5 us -> 34.9 us  [local(): pl.pallas_call(body, out_shape=(pltpu.VMEM((CX, CY, CZ), f32), pltpu.VMEM...]
where the time goes in v3:
time: 36.9 us; the launch traced here: 36.7 us
  Pallas kernels  34.9 us (95%)
  local copies, waits for them, and re-layouts  1.24 us (3%)
  between operations  0.64 us (2%)
    pallas_call x1, Pallas kernels, local(): pl.pallas_call(body, out_shape=(pltpu.VMEM((CX, CY, CZ), f32), pltpu.VMEM...  34.9 us
    unnamed x2, local copies, waits for them, and re-layouts  1.24 us

profile of v3, /device:TPU:1, one launch (start us, length us, event | category | flops | bytes accessed | tf_op | source)
XLA Modules:
  0.0 36.7 jit_solution(6966201717111053979)
XLA Ops:
  0.6 34.9 %shard_map.59 = (f32[8,8,128]{2,1,0:T(8,128)S(1)}, f32[3,8,1,1,512]{4,3,2,1,0:T(1,128)S(1)}) custom-call(f32[8,1,1,512]{3,2,1,0:T(1,128)} %q_hbm.1, f32[3,8,1,1,512]{4,3,2,1,0:T(1,128)} %off_hbm.1, s32[2,8,1,1,512]{4,3,2,1,0:T(1,128)} %cell_hbm.1, bf16[17,17,17]{2,1,0:T(8,128)(2,1)} %kern_hbm.1), custom_call_target="tpu_custom_call" | custom-call | tf_op jit(solution)/shard_map/pallas_call | solution.py:423
  35.5 0.6 %copy.8 = f32[8,8,128]{2,1,0:T(8,128)} copy(f32[8,8,128]{2,1,0:T(8,128)S(1)} %get-tuple-element.2) | data formatting | bytes 65536
  36.1 0.6 %copy.9 = f32[3,8,1,1,512]{4,3,2,1,0:T(1,128)} copy(f32[3,8,1,1,512]{4,3,2,1,0:T(1,128)S(1)} %get-tuple-element.3) | data formatting | bytes 98304

commit v4 on v3

--- a/solution.py
+++ b/solution.py
@@ -343,7 +343,7 @@
 
     for m in range(4):
         place(hb[0:16], hb[16 + 16 * m : 32 + 16 * m], 5 + m, 1, (2 * m, 2 * m + 1))
-    for n in reversed(range(len(HALO))):
+    def receive(n):
         dx, dy = HALO[n]
         halo[n].wait_recv()
         sx, b = -dx, (1 - dy) % 4
@@ -363,7 +363,7 @@
                     4 * sx + 5 + m, b, (2 * m, 2 * m + 1),
                 )
 
-    for p in range(6):
+    def convolve(p):
         skip = 272 if p == 0 else 0
         out = mm(tb[skip:544, 0:576], w[64 * p : 64 * p + 576, :])
         for h in range(skip // 272, 2):
@@ -389,6 +389,15 @@
             phl[at : at + 16, 128:256] = tl
             if 1 <= p <= 4:
                 pot_ref[2 * p + h - 2] = main[0:8]
+
+    upward = sum(1 for dx, _ in HALO if dx > 0)
+    for n in reversed(range(upward, len(HALO))):
+        receive(n)
+    convolve(5)
+    for n in reversed(range(upward)):
+        receive(n)
+    for p in range(5):
+        convolve(p)
 
     for t in range(TILES):
         at = (t + 1) * 16
@@ -446,11 +455,11 @@
             pltpu.VMEM((8, 24, 128), f32),
             pltpu.VMEM((len(FOLD), 8, 128), f32),
             pltpu.VMEM((8, 24, 128), f32),
-            pltpu.VMEM((64, 128), f32),
+            pltpu.VMEM((72, 128), f32),
             pltpu.VMEM((96, 128), bf16),
             pltpu.VMEM((len(HALO), 80, 128), bf16),
             pltpu.VMEM((32 * 21, 128), f32),
-            pltpu.VMEM((5, 768, 128), f32),
+            pltpu.VMEM((5, 784, 128), f32),
             pltpu.VMEM((544, 640), bf16),
             pltpu.VMEM((14 * 64, 256), bf16),
             pltpu.VMEM((192, 256), bf16),

time: 36.9 us -> 37.6 us (1.019)
  Pallas kernels: 34.9 us -> 35.6 us
    pallas_call x1, Pallas kernels: 34.9 us -> 35.6 us  [local(): pl.pallas_call(body, out_shape=(pltpu.VMEM((CX, CY, CZ), f32), pltpu.VMEM...]
where the time goes in v4:
time: 37.6 us; the launch traced here: 37.4 us
  Pallas kernels  35.6 us (95%)
  local copies, waits for them, and re-layouts  1.24 us (3%)
  between operations  0.64 us (2%)
    pallas_call x1, Pallas kernels, local(): pl.pallas_call(body, out_shape=(pltpu.VMEM((CX, CY, CZ), f32), pltpu.VMEM...  35.6 us
    unnamed x2, local copies, waits for them, and re-layouts  1.24 us

profile of v4, /device:TPU:1, one launch (start us, length us, event | category | flops | bytes accessed | tf_op | source)
XLA Modules:
  0.0 37.4 jit_solution(2663079603475628271)
XLA Ops:
  0.6 35.6 %shard_map.59 = (f32[8,8,128]{2,1,0:T(8,128)S(1)}, f32[3,8,1,1,512]{4,3,2,1,0:T(1,128)S(1)}) custom-call(f32[8,1,1,512]{3,2,1,0:T(1,128)} %q_hbm.1, f32[3,8,1,1,512]{4,3,2,1,0:T(1,128)} %off_hbm.1, s32[2,8,1,1,512]{4,3,2,1,0:T(1,128)} %cell_hbm.1, bf16[17,17,17]{2,1,0:T(8,128)(2,1)} %kern_hbm.1), custom_call_target="tpu_custom_call" | custom-call | tf_op jit(solution)/shard_map/pallas_call | solution.py:432
  36.2 0.6 %copy.8 = f32[8,8,128]{2,1,0:T(8,128)} copy(f32[8,8,128]{2,1,0:T(8,128)S(1)} %get-tuple-element.2) | data formatting | bytes 65536
  36.8 0.6 %copy.9 = f32[3,8,1,1,512]{4,3,2,1,0:T(1,128)} copy(f32[3,8,1,1,512]{4,3,2,1,0:T(1,128)S(1)} %get-tuple-element.3) | data formatting | bytes 98304

commit v5 on v3

--- a/solution.py
+++ b/solution.py
@@ -177,9 +177,26 @@
         for half in range(2):
             zbuf[0, half, part] = zr[part][8 * half : 8 * half + 8]
             zbuf[1, half, part] = zl[part][8 * half : 8 * half + 8]
+    row8 = lax.broadcasted_iota(jnp.int32, (8, 128), 0)
     flat = [m for m in FOLD if m[2] == 0]
     for n, (dx, dy, _) in enumerate(flat):
         half, part = int(dy != 0), int(dx != 0)
+        if dx and dy:
+            tile = ends[part][8:16]
+            planes = (0,) if dx < 0 else (9, 10)
+            for m in reversed(range(len(planes) + 1)):
+                if m < len(planes):
+                    part_m = pm[pl.ds(16 * planes[m] + 8, 8), :]
+                else:
+                    part_m = ends[part][8:16]
+                moved = pltpu.roll(part_m, 2 * m if dy > 0 else m, 0) if m else part_m
+                if dy > 0:
+                    here = (row8 >> 1) == m
+                else:
+                    here = row8 == (7 + m) % 8
+                tile = jnp.where(here, moved, tile)
+            sbuf[n, 0:8] = tile
+            continue
         sbuf[n, 0:8] = ends[part][8 * half : 8 * half + 8]
         if dx == 0:
             rows = (15,) if dy < 0 else (8, 9)
@@ -200,7 +217,7 @@
             dst = rz.at[n]
         else:
             m = flat.index((dx, dy, dz))
-            rows = 16 if (dx < 0 or (dx == 0 and dy < 0)) else 24
+            rows = 8 if dx and dy else 16 if dx < 0 or dy < 0 else 24
             src = sbuf.at[m, pl.ds(0, rows)]
             dst = r0.at[m, pl.ds(0, rows)]
         copy = pltpu.make_async_remote_copy(
@@ -226,7 +243,6 @@
     for copy in fold:
         copy.wait_recv()
 
-    row8 = lax.broadcasted_iota(jnp.int32, (8, 128), 0)
     lane8 = lax.broadcasted_iota(jnp.int32, (8, 128), 1)
     slot8 = lane8 // 16
     index8 = lane8 & 15
@@ -252,6 +268,15 @@
             high_end = high_end + slots_of(dx, rows_of(dy, rz[n]))
         else:
             m = flat.index((dx, dy, dz))
+            if dx and dy:
+                step = 2 if dy > 0 else 1
+                count = 3 if dx > 0 else 2
+                got = [r0[m, 0:8]] + [pltpu.roll(r0[m, 0:8], 8 - step * j, 0) for j in range(1, count)]
+                got = [rows_of(dy, value) for value in got]
+                own_end = own_end + slots_of(dx, got[-1])
+                for x, value in zip((0, 1) if dx > 0 else (7,), got):
+                    plane[x] = plane[x] + value
+                continue
             own_end = own_end + slots_of(dx, rows_of(dy, r0[m, 0:8]))
             if dx > 0:
                 plane[0] = plane[0] + rows_of(dy, r0[m, 8:16])
@@ -446,11 +471,11 @@
             pltpu.VMEM((8, 24, 128), f32),
             pltpu.VMEM((len(FOLD), 8, 128), f32),
             pltpu.VMEM((8, 24, 128), f32),
-            pltpu.VMEM((64, 128), f32),
+            pltpu.VMEM((72, 128), f32),
             pltpu.VMEM((96, 128), bf16),
             pltpu.VMEM((len(HALO), 80, 128), bf16),
             pltpu.VMEM((32 * 21, 128), f32),
-            pltpu.VMEM((5, 768, 128), f32),
+            pltpu.VMEM((5, 784, 128), f32),
             pltpu.VMEM((544, 640), bf16),
             pltpu.VMEM((14 * 64, 256), bf16),
             pltpu.VMEM((192, 256), bf16),

time: 36.9 us -> 36.9 us (level)
  no operation moved by 1% of the time
where the time goes in v5:
time: 36.9 us; the launch traced here: 36.8 us
  Pallas kernels  34.9 us (95%)
  local copies, waits for them, and re-layouts  1.24 us (3%)
  between operations  0.64 us (2%)
    pallas_call x1, Pallas kernels, local(): pl.pallas_call(body, out_shape=(pltpu.VMEM((CX, CY, CZ), f32), pltpu.VMEM...  34.9 us
    unnamed x2, local copies, waits for them, and re-layouts  1.24 us

profile of v5, /device:TPU:1, one launch (start us, length us, event | category | flops | bytes accessed | tf_op | source)
XLA Modules:
  0.0 36.8 jit_solution(3089928433880868771)
XLA Ops:
  0.6 34.9 %shard_map.59 = (f32[8,8,128]{2,1,0:T(8,128)S(1)}, f32[3,8,1,1,512]{4,3,2,1,0:T(1,128)S(1)}) custom-call(f32[8,1,1,512]{3,2,1,0:T(1,128)} %q_hbm.1, f32[3,8,1,1,512]{4,3,2,1,0:T(1,128)} %off_hbm.1, s32[2,8,1,1,512]{4,3,2,1,0:T(1,128)} %cell_hbm.1, bf16[17,17,17]{2,1,0:T(8,128)(2,1)} %kern_hbm.1), custom_call_target="tpu_custom_call" | custom-call | tf_op jit(solution)/shard_map/pallas_call | solution.py:448
  35.5 0.6 %copy.8 = f32[8,8,128]{2,1,0:T(8,128)} copy(f32[8,8,128]{2,1,0:T(8,128)S(1)} %get-tuple-element.2) | data formatting | bytes 65536
  36.1 0.6 %copy.9 = f32[3,8,1,1,512]{4,3,2,1,0:T(1,128)} copy(f32[3,8,1,1,512]{4,3,2,1,0:T(1,128)S(1)} %get-tuple-element.3) | data formatting | bytes 98304

commit v6 on v5

--- a/solution.py
+++ b/solution.py
@@ -388,7 +388,7 @@
                     4 * sx + 5 + m, b, (2 * m, 2 * m + 1),
                 )
 
-    for p in range(6):
+    def convolve(p):
         skip = 272 if p == 0 else 0
         out = mm(tb[skip:544, 0:576], w[64 * p : 64 * p + 576, :])
         for h in range(skip // 272, 2):
@@ -415,7 +415,7 @@
             if 1 <= p <= 4:
                 pot_ref[2 * p + h - 2] = main[0:8]
 
-    for t in range(TILES):
+    def interpolate(t):
         at = (t + 1) * 16
         high = phh[at : at + 64, 0:ZROWS]
         both = jnp.concatenate([high, phl[at : at + 64, 0:ZROWS]], axis=0)
@@ -435,6 +435,12 @@
         frc_ref[0, t, 0] = jnp.sum(fx * wy, axis=0, keepdims=True)
         frc_ref[1, t, 0] = -jnp.sum(fy * sy, axis=0, keepdims=True)
         frc_ref[2, t, 0] = -jnp.sum(fz * wy, axis=0, keepdims=True)
+
+    for p in range(6):
+        convolve(p)
+        if p >= 2:
+            interpolate(2 * p - 4)
+            interpolate(2 * p - 3)
 
     for copy in fold:
         copy.wait_send()

time: 36.9 us -> 37.8 us (1.024)
  Pallas kernels: 34.9 us -> 35.7 us
    pallas_call x1, Pallas kernels: 34.9 us -> 35.7 us  [local(): pl.pallas_call(body, out_shape=(pltpu.VMEM((CX, CY, CZ), f32), pltpu.VMEM...]
where the time goes in v6:
time: 37.8 us; the launch traced here: 37.6 us
  Pallas kernels  35.7 us (94%)
  local copies, waits for them, and re-layouts  1.24 us (3%)
  between operations  0.64 us (2%)
    pallas_call x1, Pallas kernels, local(): pl.pallas_call(body, out_shape=(pltpu.VMEM((CX, CY, CZ), f32), pltpu.VMEM...  35.7 us
    unnamed x2, local copies, waits for them, and re-layouts  1.24 us

profile of v6, /device:TPU:1, one launch (start us, length us, event | category | flops | bytes accessed | tf_op | source)
XLA Modules:
  0.0 37.6 jit_solution(3562223900854149647)
XLA Ops:
  0.6 35.7 %shard_map.59 = (f32[8,8,128]{2,1,0:T(8,128)S(1)}, f32[3,8,1,1,512]{4,3,2,1,0:T(1,128)S(1)}) custom-call(f32[8,1,1,512]{3,2,1,0:T(1,128)} %q_hbm.1, f32[3,8,1,1,512]{4,3,2,1,0:T(1,128)} %off_hbm.1, s32[2,8,1,1,512]{4,3,2,1,0:T(1,128)} %cell_hbm.1, bf16[17,17,17]{2,1,0:T(8,128)(2,1)} %kern_hbm.1), custom_call_target="tpu_custom_call" | custom-call | tf_op jit(solution)/shard_map/pallas_call | solution.py:454
  36.4 0.6 %copy.8 = f32[8,8,128]{2,1,0:T(8,128)} copy(f32[8,8,128]{2,1,0:T(8,128)S(1)} %get-tuple-element.2) | data formatting | bytes 65536
  37.0 0.6 %copy.9 = f32[3,8,1,1,512]{4,3,2,1,0:T(1,128)} copy(f32[3,8,1,1,512]{4,3,2,1,0:T(1,128)S(1)} %get-tuple-element.3) | data formatting | bytes 98304
